TPU v7x, 32 devices: a whole 2x2x4 slice. The times are simulated.
32 devices in a mesh: cells: 8 (over z, y), freq: 4 (over x, core).
Axes of the slice: x: 2, y: 2, z: 4, core: 2. Of those that a mesh axis runs over, the one named last changes fastest.
Arguments:
- adj_source: float32 [4, 2, 32768], P('freq', None, 'cells'), may hold values from -6 to 6
- contrast: float32 [4, 32768], P('freq', 'cells'), may hold values from 0.2 to 0.8
- background: float32 [4, 2, 32768], P('freq', None, 'cells'), may hold values from -6 to 6
- near_blocks: float32 [4, 2, 192, 32768], P('freq', None, None, 'cells'), may hold values from -0.3125 to 0.3125
- near_list: int32 [512, 3], P('cells'), may hold values from 0 to 511, as said below
- proj_basis: float32 [4, 2, 16, 32768], P('freq', None, None, 'cells'), may hold values from -0.5 to 0.5
- expand_basis: float32 [4, 2, 16, 32768], P('freq', None, None, 'cells'), may hold values from -1 to 1
- coupling: float32 [4, 2, 16, 16, 8192], P('freq', None, None, None, 'cells'), may hold values from -0.25 to 0.25
- far_owner: int32 [8192, 1], P('cells'), may hold values from 0 to 7; in each aligned block of 1024 rows (0 to 1023, 1024 to 2047, ...) at most 256 rows name the same one
- far_slot: int32 [8192], P('cells'), may hold values from 0 to 63
Outputs:
- adjoint: float32 [4, 2, 32768], P('freq', None, 'cells')
- gradient: float32 [32768], P('cells')
Inputs may be any that keep to these rules, and one draw needn't show every extreme that they name: near_list[c, 0] = c, and every partner of c lies on the same device: near_list[c, k] // 64 == c // 64. `far_owner`: among the far pairs of one device's targets (aligned blocks of 1024 rows) at most 256 have sources on any one device.
All inputs are finite; a program needn't handle non-finite values.
Results may differ from a plain program's by a relative error of at most 0.0001.
Values sent between devices are 32-bit elements; how exact they have to be, the bound alone decides.
A program may use at most 64 MiB of HBM per device.

v0:
```python
import functools

import jax
import jax.numpy as jnp
from jax import lax
from jax.experimental import pallas as pl
from jax.experimental.pallas import tpu as pltpu
from jax.sharding import PartitionSpec as P

ITERS = 2
LANES = 128
MESH = pl.DeviceIdType.MESH
F32 = jnp.float32
BF16 = jnp.bfloat16


def split(x):
    high = x.astype(BF16)
    return high, (x - high.astype(F32)).astype(BF16)


def dot(a, b):
    return jnp.dot(a, b, preferred_element_type=F32)


def onehot(mask):
    return jnp.where(mask, 1.0, 0.0).astype(BF16)


def kernel(
    dims,
    adj_hbm,
    con_hbm,
    back_hbm,
    near_hbm,
    list_ref,
    proj_hbm,
    exp_hbm,
    coup_hbm,
    owner_ref,
    slot_ref,
    out_hbm,
    grad_ref,
    adj,
    con,
    back,
    near,
    proj,
    expand,
    coup,
    rows,
    spread,
    collect,
    pick_near,
    pick_far,
    pair_sum,
    acc,
    qbuf,
    gbuf,
    field,
    in_sem,
    near_sem,
    out_sem,
    send_sem,
    recv_sem,
    gsend_sem,
    grecv_sem,
):
    peers, freqs, clusters, cells, rank, near_count, pairs, near_parts = dims
    width = cells // clusters
    shift = width.bit_length() - 1
    half = LANES // 2
    lines = cells // LANES
    far_count = pairs // clusters
    far_shift = far_count.bit_length() - 1
    me = lax.axis_index("cells")
    my_f = lax.axis_index("freq")

    ins = [
        pltpu.make_async_copy(src, dst, in_sem.at[i])
        for i, (src, dst) in enumerate(
            [(con_hbm, con), (adj_hbm, adj), (proj_hbm, proj), (coup_hbm, coup), (exp_hbm, expand), (back_hbm, back)]
        )
    ]
    con_in, adj_in, proj_in, coup_in, exp_in, back_in = ins
    part = cells // near_parts
    near_in = [
        pltpu.make_async_copy(
            near_hbm.at[:, :, pl.ds(i * part, part)], near.at[:, :, pl.ds(i * part, part)], near_sem.at[i]
        )
        for i in range(near_parts)
    ]
    con_in.start()
    adj_in.start()
    proj_in.start()
    for c in near_in:
        c.start()
    coup_in.start()
    exp_in.start()
    back_in.start()

    barrier = pltpu.get_barrier_semaphore()
    for d in range(1, peers):
        pl.semaphore_signal(barrier, inc=1, device_id={"cells": lax.rem(me + d, peers)}, device_id_type=MESH)
    for d in range(1, freqs):
        pl.semaphore_signal(barrier, inc=1, device_id={"freq": lax.rem(my_f + d, freqs)}, device_id_type=MESH)

    step = 512
    for t in range(0, cells, step):
        r = lax.broadcasted_iota(jnp.int32, (LANES, step), 0) & (half - 1)
        c = (lax.broadcasted_iota(jnp.int32, (LANES, step), 1) + t) >> shift
        spread[:, t : t + step] = onehot(r == c)
        r = (lax.broadcasted_iota(jnp.int32, (step, LANES), 0) + t) >> shift
        c = lax.broadcasted_iota(jnp.int32, (step, LANES), 1) & (half - 1)
        collect[t : t + step, :] = onehot(r == c)

    lane64 = lax.broadcasted_iota(jnp.int32, (rank, LANES), 1) < half

    def weigh():
        w = field[:, :] * con[:, :]
        high = w.astype(BF16).astype(F32)
        low = w - high
        for ri in range(2):
            for m in range(lines):
                rows[ri * lines + m : ri * lines + m + 1, :] = high[ri : ri + 1, m * LANES : (m + 1) * LANES]
                rows[(2 + ri) * lines + m : (2 + ri) * lines + m + 1, :] = low[ri : ri + 1, m * LANES : (m + 1) * LANES]
        return w

    def project(w, it):
        total = jnp.zeros((4 * rank, LANES), F32)
        for t in range(0, cells, step):
            wr, wi = w[0:1, t : t + step], w[1:2, t : t + step]
            pr, pi = proj[0, :, t : t + step], proj[1, :, t : t + step]
            re_h, re_l = split(pr * wr - pi * wi)
            im_h, im_l = split(pr * wi + pi * wr)
            x = jnp.concatenate([re_h, im_h, re_l, im_l], axis=0)
            total += dot(x, collect[t : t + step, :])
        q = total[: 2 * rank] + total[2 * rank :]
        qbuf[it, me] = jnp.where(lane64, q[:rank], q[rank:])

    def send(it):
        sends = []
        for d in range(1, peers):
            copy = pltpu.make_async_remote_copy(
                src_ref=qbuf.at[it, me],
                dst_ref=qbuf.at[it, me],
                send_sem=send_sem.at[it, d],
                recv_sem=recv_sem.at[it, d],
                device_id={"cells": lax.rem(me + d, peers)},
                device_id_type=MESH,
            )
            copy.start()
            sends.append(copy)
        return sends

    def near_field(it):
        turned = rows[:, :].T.astype(BF16)
        left = jnp.concatenate([turned[:width], turned[width:]], axis=1)
        got = dot(left, pick_near[:, :])
        lane = lax.broadcasted_iota(jnp.int32, (width, LANES), 1) < half
        parts = []
        for b in range(2 * near_count):
            g = got[:, b * LANES : (b + 1) * LANES]
            high = g.astype(BF16).astype(F32)
            parts.append(jnp.where(lane, high, g - high).astype(BF16))
        lhs = jnp.concatenate(parts, axis=0)
        deep = near_count * width
        chunk = 256

        def one(t):
            at = pl.ds(pl.multiple_of(t * chunk, chunk), chunk)
            wide = dot(lhs, spread[:, at])
            re = jnp.zeros((8, chunk), F32)
            im = jnp.zeros((8, chunk), F32)
            for j in range(0, deep, 8):
                br, bi = near[0, j : j + 8, at], near[1, j : j + 8, at]
                wr, wi = wide[j : j + 8], wide[deep + j : deep + j + 8]
                re += br * wr - bi * wi
                im += br * wi + bi * wr
            acc[0, :, at] = re
            acc[1, :, at] = im

        per = part // chunk
        if it == 0:
            for i in range(near_parts):
                near_in[i].wait()
                pl.loop(i * per, (i + 1) * per)(one)
        else:
            pl.loop(0, cells // chunk)(one)

    def far_field(it, sends):
        for c in sends:
            c.wait_recv()
        re, im = [], []
        for m in range(0, peers, 2):
            a, b = qbuf[it, m], qbuf[it, m + 1]
            re.append(jnp.where(lane64, a, pltpu.roll(b, half, 1)))
            im.append(jnp.where(lane64, pltpu.roll(a, half, 1), b))
        q = jnp.concatenate([jnp.concatenate(re, axis=1), jnp.concatenate(im, axis=1)], axis=0)
        q_h, q_l = split(q)
        got = dot(jnp.concatenate([q_h, q_l], axis=0), pick_far[:, :])
        got = got[: 2 * rank] + got[2 * rank :]
        qr, qi = got[:rank], got[rank:]
        if it == 0:
            coup_in.wait()
        sums = jnp.zeros((2 * rank * 8, LANES), F32)
        wide = 256
        for t in range(0, pairs, wide):
            res, ims = [], []
            a, b = qr[:, t : t + wide], qi[:, t : t + wide]
            for o in range(rank):
                cr, ci = coup[0, o, :, t : t + wide], coup[1, o, :, t : t + wide]
                x = cr * a - ci * b
                y = cr * b + ci * a
                res.append(sum(x[k : k + 8] for k in range(0, rank, 8)))
                ims.append(sum(y[k : k + 8] for k in range(0, rank, 8)))
            high, low = split(jnp.concatenate(res + ims, axis=0))
            sel = pair_sum[t : t + wide, :]
            sums += dot(high, sel) + dot(low, sel)
        z = jnp.sum(sums.reshape(2 * rank, 8, LANES), axis=1)
        z_high = z.astype(BF16).astype(F32)
        lane = lax.broadcasted_iota(jnp.int32, (2 * rank, LANES), 1) < half
        z = jnp.where(lane, z_high, z - z_high).astype(BF16)
        if it == 0:
            exp_in.wait()
        for t in range(0, cells, step):
            wide_z = dot(z, spread[:, t : t + step])
            zr, zi = wide_z[:rank], wide_z[rank:]
            er, ei = expand[0, :, t : t + step], expand[1, :, t : t + step]
            x = er * zr - ei * zi
            y = er * zi + ei * zr
            x = acc[0, :, t : t + step] + sum(x[k : k + 8] for k in range(0, rank, 8))
            y = acc[1, :, t : t + step] + sum(y[k : k + 8] for k in range(0, rank, 8))
            new = jnp.concatenate([jnp.sum(x, axis=0, keepdims=True), jnp.sum(y, axis=0, keepdims=True)], axis=0)
            field[:, t : t + step] = adj[:, t : t + step] + new

    con_in.wait()
    adj_in.wait()
    field[:, :] = adj[:, :]
    w = weigh()
    proj_in.wait()
    project(w, 0)
    pl.semaphore_wait(barrier, peers + freqs - 2)
    sends = send(0)
    everyone = sends

    r = lax.broadcasted_iota(jnp.int32, (2 * LANES, LANES), 0)
    lbits = lines.bit_length() - 1
    cluster = ((r & (lines - 1)) << 1) + (r >> 7)
    source_ri = (r >> lbits) & 1
    local = list_ref[:, :] - me * clusters
    local = jnp.concatenate([local, local], axis=1)
    for ri in range(2):
        for k in range(near_count):
            b = ri * near_count + k
            pick_near[:, b * LANES : (b + 1) * LANES] = onehot((cluster == local[k : k + 1, :]) & (source_ri == ri))
    near_field(0)

    source = owner_ref[:, :] * clusters + slot_ref[:, :]

    @pl.loop(0, peers * clusters // 64)
    def _(i):
        r = lax.broadcasted_iota(jnp.int32, (64, pairs), 0) + i * 64
        pick_far[pl.ds(pl.multiple_of(i * 64, 64), 64), :] = onehot(r == source)

    r = lax.broadcasted_iota(jnp.int32, (pairs, LANES), 0) >> far_shift
    c = lax.broadcasted_iota(jnp.int32, (pairs, LANES), 1) & (half - 1)
    pair_sum[:, :] = onehot(r == c)

    far_field(0, sends)
    for it in range(1, ITERS):
        w = weigh()
        project(w, it)
        sends = send(it)
        everyone = everyone + sends
        near_field(it)
        far_field(it, sends)

    out_copy = pltpu.make_async_copy(field, out_hbm, out_sem)
    out_copy.start()
    back_in.wait()
    terms = back[:, :] * field[:, :]
    terms = terms[0:1] + terms[1:2]
    for m in range(lines):
        gbuf[0, m : m + 1, :] = terms[:, m * LANES : (m + 1) * LANES]
    gsends = []
    for d in range(1, freqs):
        copy = pltpu.make_async_remote_copy(
            src_ref=gbuf.at[0],
            dst_ref=gbuf.at[d],
            send_sem=gsend_sem.at[d],
            recv_sem=grecv_sem.at[d],
            device_id={"freq": lax.rem(my_f + d, freqs)},
            device_id_type=MESH,
        )
        copy.start()
        gsends.append(copy)
    for c in everyone:
        c.wait_send()
    total = gbuf[0]
    for d, c in enumerate(gsends):
        c.wait_recv()
        total += gbuf[d + 1]
    grad_ref[:, :] = total
    for c in gsends:
        c.wait_send()
    out_copy.wait()


def per_device(
    peers,
    freqs,
    adj_source,
    contrast,
    background,
    near_blocks,
    near_list,
    proj_basis,
    expand_basis,
    coupling,
    far_owner,
    far_slot,
):
    clusters, near_count = near_list.shape
    cells = contrast.shape[1]
    rank = proj_basis.shape[2]
    pairs = far_slot.shape[0]
    lines = cells // LANES
    near_parts = 4
    dims = (peers, freqs, clusters, cells, rank, near_count, pairs, near_parts)
    hbm = pl.BlockSpec(memory_space=pl.ANY)
    vmem = pl.BlockSpec(memory_space=pltpu.VMEM)
    deep = near_blocks.shape[2]
    adjoint, gradient = pl.pallas_call(
        functools.partial(kernel, dims),
        out_shape=(
            jax.ShapeDtypeStruct((2, cells), F32),
            jax.ShapeDtypeStruct((lines, LANES), F32),
        ),
        in_specs=[hbm, hbm, hbm, hbm, vmem, hbm, hbm, hbm, vmem, vmem],
        out_specs=(hbm, vmem),
        scratch_shapes=[
            pltpu.VMEM((2, cells), F32),
            pltpu.VMEM((1, cells), F32),
            pltpu.VMEM((2, cells), F32),
            pltpu.VMEM((2, deep, cells), F32),
            pltpu.VMEM((2, rank, cells), F32),
            pltpu.VMEM((2, rank, cells), F32),
            pltpu.VMEM((2, rank, rank, pairs), F32),
            pltpu.VMEM((4 * lines, LANES), F32),
            pltpu.VMEM((LANES, cells), BF16),
            pltpu.VMEM((cells, LANES), BF16),
            pltpu.VMEM((2 * LANES, 2 * near_count * LANES), BF16),
            pltpu.VMEM((peers * clusters, pairs), BF16),
            pltpu.VMEM((pairs, LANES), BF16),
            pltpu.VMEM((2, 8, cells), F32),
            pltpu.VMEM((ITERS, peers, rank, LANES), F32),
            pltpu.VMEM((freqs, lines, LANES), F32),
            pltpu.VMEM((2, cells), F32),
            pltpu.SemaphoreType.DMA((6,)),
            pltpu.SemaphoreType.DMA((near_parts,)),
            pltpu.SemaphoreType.DMA,
            pltpu.SemaphoreType.DMA((ITERS, peers)),
            pltpu.SemaphoreType.DMA((ITERS, peers)),
            pltpu.SemaphoreType.DMA((freqs,)),
            pltpu.SemaphoreType.DMA((freqs,)),
        ],
        compiler_params=pltpu.CompilerParams(
            collective_id=0, has_side_effects=True, vmem_limit_bytes=48 * 2**20
        ),
    )(
        adj_source[0],
        contrast,
        background[0],
        near_blocks[0],
        near_list.T,
        proj_basis[0],
        expand_basis[0],
        coupling[0],
        far_owner.reshape(1, pairs),
        far_slot.reshape(1, pairs),
    )
    return adjoint[None], gradient.reshape(cells)


def solution(mesh):
    return jax.shard_map(
        functools.partial(per_device, mesh.shape["cells"], mesh.shape["freq"]),
        mesh=mesh,
        in_specs=(
            P("freq", None, "cells"),
            P("freq", "cells"),
            P("freq", None, "cells"),
            P("freq", None, None, "cells"),
            P("cells", None),
            P("freq", None, None, "cells"),
            P("freq", None, None, "cells"),
            P("freq", None, None, None, "cells"),
            P("cells", None),
            P("cells"),
        ),
        out_specs=(P("freq", None, "cells"), P("cells")),
        check_vma=False,
    )
```

profile of v0, /device:TPU:0, one launch (start us, length us, event | category | flops | bytes accessed | tf_op | source)
XLA Modules:
  0.0 30.8 jit_solution(5839109910087645826)
XLA Ops:
  0.6 0.0 copy-start
  0.6 1.6 %copy-done = f32[1,2,16,16,1024]{4,3,2,1,0:T(8,128)S(1)} copy-done((f32[1,2,16,16,1024]{4,3,2,1,0:T(8,128)S(1)}, f32[1,2,16,16,1024]{4,3,2,1,0:T(8,128)}, u32[]{:S(2)}) %copy-start) | copy-done | bytes 2097176
  2.2 0.0 copy-start.1
  2.2 1.0 %copy-done.1 = f32[1,2,16,4096]{3,2,1,0:T(8,128)S(1)} copy-done((f32[1,2,16,4096]{3,2,1,0:T(8,128)S(1)}, f32[1,2,16,4096]{3,2,1,0:T(8,128)}, u32[]{:S(2)}) %copy-start.1) | copy-done | bytes 524312
  3.3 0.0 copy-start.2
  3.3 1.0 %copy-done.2 = f32[1,2,16,4096]{3,2,1,0:T(8,128)S(1)} copy-done((f32[1,2,16,4096]{3,2,1,0:T(8,128)S(1)}, f32[1,2,16,4096]{3,2,1,0:T(8,128)}, u32[]{:S(2)}) %copy-start.2) | copy-done | bytes 524312
  4.3 0.0 copy-start.3
  4.3 0.8 %copy-done.3 = f32[1,2,4096]{2,1,0:T(2,128)S(1)} copy-done((f32[1,2,4096]{2,1,0:T(2,128)S(1)}, f32[1,2,4096]{2,1,0:T(2,128)}, u32[]{:S(2)}) %copy-start.3) | copy-done | bytes 32792
  5.1 0.0 copy-start.4
  5.1 0.8 %copy-done.4 = f32[1,2,4096]{2,1,0:T(2,128)S(1)} copy-done((f32[1,2,4096]{2,1,0:T(2,128)S(1)}, f32[1,2,4096]{2,1,0:T(2,128)}, u32[]{:S(2)}) %copy-start.4) | copy-done | bytes 32792
  5.8 0.0 copy-start.5
  5.8 0.7 %copy-done.5 = f32[1,4096]{1,0:T(1,128)S(1)} copy-done((f32[1,4096]{1,0:T(1,128)S(1)}, f32[1,4096]{1,0:T(1,128)}, u32[]{:S(2)}) %copy-start.5) | copy-done | bytes 16408
  6.5 0.0 copy-start.6
  6.5 0.7 %copy-done.6 = s32[1024,1]{0,1:T(1,128)S(1)} copy-done((s32[1024,1]{0,1:T(1,128)S(1)}, s32[1024,1]{0,1:T(1,128)}, u32[]{:S(2)}) %copy-start.6) | copy-done | bytes 4120
  7.2 0.0 copy-start.7
  7.2 0.7 %copy-done.7 = s32[1024]{0:T(1024)S(1)} copy-done((s32[1024]{0:T(1024)S(1)}, s32[1024]{0:T(1024)}, u32[]{:S(2)}) %copy-start.7) | copy-done | bytes 4120
  7.9 0.0 copy-start.8
  7.9 0.7 %copy-done.8 = s32[64,3]{0,1:T(4,128)S(1)} copy-done((s32[64,3]{0,1:T(4,128)S(1)}, s32[64,3]{0,1:T(4,128)}, u32[]{:S(2)}) %copy-start.8) | copy-done | bytes 792
  8.6 21.0 %shard_map.113 = (f32[2,4096]{1,0:T(2,128)S(1)}, f32[32,128]{1,0:T(8,128)S(1)}) custom-call(f32[2,4096]{1,0:T(2,128)S(1)} %bitcast.14, f32[1,4096]{1,0:T(1,128)S(1)} %copy-done.5, f32[2,4096]{1,0:T(2,128)S(1)} %bitcast.15, f32[2,192,4096]{2,1,0:T(8,128)} %bitcast.21, s32[3,64]{1,0:T(4,128)S(1)} %bitcast.20, f32[2,16,4096]{2,1,0:T(8,128)S(1)} %bitcast.12, ...), custom_call_target="tpu_custom_call" | custom-call | tf_op jit(solution)/shard_map/pallas_call | solution.py:334
  29.6 0.6 %copy.14 = f32[1,2,4096]{2,1,0:T(2,128)} copy(f32[1,2,4096]{2,1,0:T(2,128)S(1)} %bitcast.16) | data formatting | bytes 65536
  30.2 0.6 %copy.15 = f32[4096]{0:T(1024)} copy(f32[4096]{0:T(1024)S(1)} %bitcast.17) | data formatting | bytes 32768
Async XLA Ops:
  0.6 1.6 %copy-start = (f32[1,2,16,16,1024]{4,3,2,1,0:T(8,128)S(1)}, f32[1,2,16,16,1024]{4,3,2,1,0:T(8,128)}, u32[]{:S(2)}) copy-start(f32[1,2,16,16,1024]{4,3,2,1,0:T(8,128)} %param.17) | copy-start | bytes 6291460
  2.2 1.0 %copy-start.1 = (f32[1,2,16,4096]{3,2,1,0:T(8,128)S(1)}, f32[1,2,16,4096]{3,2,1,0:T(8,128)}, u32[]{:S(2)}) copy-start(f32[1,2,16,4096]{3,2,1,0:T(8,128)} %param.15) | copy-start | bytes 1572868
  3.3 1.0 %copy-start.2 = (f32[1,2,16,4096]{3,2,1,0:T(8,128)S(1)}, f32[1,2,16,4096]{3,2,1,0:T(8,128)}, u32[]{:S(2)}) copy-start(f32[1,2,16,4096]{3,2,1,0:T(8,128)} %param.16) | copy-start | bytes 1572868
  4.3 0.8 %copy-start.3 = (f32[1,2,4096]{2,1,0:T(2,128)S(1)}, f32[1,2,4096]{2,1,0:T(2,128)}, u32[]{:S(2)}) copy-start(f32[1,2,4096]{2,1,0:T(2,128)} %param.10) | copy-start | bytes 98308
  5.1 0.8 %copy-start.4 = (f32[1,2,4096]{2,1,0:T(2,128)S(1)}, f32[1,2,4096]{2,1,0:T(2,128)}, u32[]{:S(2)}) copy-start(f32[1,2,4096]{2,1,0:T(2,128)} %param.12) | copy-start | bytes 98308
  5.8 0.7 %copy-start.5 = (f32[1,4096]{1,0:T(1,128)S(1)}, f32[1,4096]{1,0:T(1,128)}, u32[]{:S(2)}) copy-start(f32[1,4096]{1,0:T(1,128)} %con_hbm.1) | copy-start | bytes 49156
  6.5 0.7 %copy-start.6 = (s32[1024,1]{0,1:T(1,128)S(1)}, s32[1024,1]{0,1:T(1,128)}, u32[]{:S(2)}) copy-start(s32[1024,1]{0,1:T(1,128)} %param.18) | copy-start | bytes 12292
  7.2 0.7 %copy-start.7 = (s32[1024]{0:T(1024)S(1)}, s32[1024]{0:T(1024)}, u32[]{:S(2)}) copy-start(s32[1024]{0:T(1024)} %param.19) | copy-start | bytes 12292
  7.9 0.7 %copy-start.8 = (s32[64,3]{0,1:T(4,128)S(1)}, s32[64,3]{0,1:T(4,128)}, u32[]{:S(2)}) copy-start(s32[64,3]{0,1:T(4,128)} %param.14) | copy-start | bytes 2308
where the time goes:
time: 31.3 us; the launch traced here: 30.8 us
  Pallas kernels  21 us (67%)
  local copies, waits for them, and re-layouts  9.18 us (29%)
  between operations  0.66 us (2%)
    pallas_call x1, Pallas kernels, per_device(): pl.pallas_call(functools.partial(kernel, dims), out_shape=(jax.ShapeDtype...  21 us
    unnamed x20, local copies, waits for them, and re-layouts  9.18 us

commit v1 on v0

--- a/solution.py
+++ b/solution.py
@@ -33,12 +33,12 @@
     con_hbm,
     back_hbm,
     near_hbm,
-    list_ref,
+    list_hbm,
     proj_hbm,
     exp_hbm,
     coup_hbm,
-    owner_ref,
-    slot_ref,
+    owner_hbm,
+    slot_hbm,
     out_hbm,
     grad_ref,
     adj,
@@ -48,10 +48,17 @@
     proj,
     expand,
     coup,
+    list_ref,
+    owner_ref,
+    slot_ref,
     rows,
+    wbuf,
     spread,
     collect,
     pick_near,
+    left,
+    block_h,
+    block_l,
     pick_far,
     pair_sum,
     acc,
@@ -79,10 +86,10 @@
     ins = [
         pltpu.make_async_copy(src, dst, in_sem.at[i])
         for i, (src, dst) in enumerate(
-            [(con_hbm, con), (adj_hbm, adj), (proj_hbm, proj), (coup_hbm, coup), (exp_hbm, expand), (back_hbm, back)]
+            [(con_hbm, con), (adj_hbm, adj), (proj_hbm, proj), (coup_hbm, coup), (exp_hbm, expand), (back_hbm, back), (list_hbm, list_ref), (owner_hbm, owner_ref), (slot_hbm, slot_ref)]
         )
     ]
-    con_in, adj_in, proj_in, coup_in, exp_in, back_in = ins
+    con_in, adj_in, proj_in, coup_in, exp_in, back_in, list_in, owner_in, slot_in = ins
     part = cells // near_parts
     near_in = [
         pltpu.make_async_copy(
@@ -93,6 +100,9 @@
     con_in.start()
     adj_in.start()
     proj_in.start()
+    list_in.start()
+    owner_in.start()
+    slot_in.start()
     for c in near_in:
         c.start()
     coup_in.start()
@@ -117,19 +127,15 @@
     lane64 = lax.broadcasted_iota(jnp.int32, (rank, LANES), 1) < half
 
     def weigh():
-        w = field[:, :] * con[:, :]
-        high = w.astype(BF16).astype(F32)
-        low = w - high
+        wbuf[:, :] = field[:, :] * con[:, :]
         for ri in range(2):
             for m in range(lines):
-                rows[ri * lines + m : ri * lines + m + 1, :] = high[ri : ri + 1, m * LANES : (m + 1) * LANES]
-                rows[(2 + ri) * lines + m : (2 + ri) * lines + m + 1, :] = low[ri : ri + 1, m * LANES : (m + 1) * LANES]
-        return w
-
-    def project(w, it):
+                rows[ri * lines + m : ri * lines + m + 1, :] = wbuf[ri : ri + 1, m * LANES : (m + 1) * LANES]
+
+    def project(it):
         total = jnp.zeros((4 * rank, LANES), F32)
         for t in range(0, cells, step):
-            wr, wi = w[0:1, t : t + step], w[1:2, t : t + step]
+            wr, wi = wbuf[0:1, t : t + step], wbuf[1:2, t : t + step]
             pr, pi = proj[0, :, t : t + step], proj[1, :, t : t + step]
             re_h, re_l = split(pr * wr - pi * wi)
             im_h, im_l = split(pr * wi + pi * wr)
@@ -154,39 +160,35 @@
         return sends
 
     def near_field(it):
-        turned = rows[:, :].T.astype(BF16)
-        left = jnp.concatenate([turned[:width], turned[width:]], axis=1)
-        got = dot(left, pick_near[:, :])
-        lane = lax.broadcasted_iota(jnp.int32, (width, LANES), 1) < half
-        parts = []
-        for b in range(2 * near_count):
-            g = got[:, b * LANES : (b + 1) * LANES]
-            high = g.astype(BF16).astype(F32)
-            parts.append(jnp.where(lane, high, g - high).astype(BF16))
-        lhs = jnp.concatenate(parts, axis=0)
-        deep = near_count * width
-        chunk = 256
+        first = lax.broadcasted_iota(jnp.int32, (4 * lines, LANES), 1) < half
+        lined = rows[:, :]
+        high = lined.astype(BF16).astype(F32)
+        lined = jnp.concatenate([high, lined - high], axis=0)
+        swapped = pltpu.roll(lined, half, 1)
+        values = jnp.concatenate([jnp.where(first, lined, swapped), jnp.where(first, swapped, lined)], axis=0)
+        values = values.astype(BF16)
+        got = [dot(pick_near[k], values) for k in range(near_count)]
+        first = lax.broadcasted_iota(jnp.int32, (4 * clusters, LANES), 1) < half
+        left[:, :LANES] = jnp.where(first, got[0], got[1]).astype(BF16)
+        left[:, LANES:] = got[2][:, :width].astype(BF16)
+        chunk = 4 * width
+        r = lax.broadcasted_iota(jnp.int32, (8, chunk), 0)
+        c = lax.broadcasted_iota(jnp.int32, (8, chunk), 1) >> shift
+        mine = (r & 3) == c
+        upper = r < 4
+        zero = jnp.zeros((8, chunk), F32)
 
         def one(t):
             at = pl.ds(pl.multiple_of(t * chunk, chunk), chunk)
-            wide = dot(lhs, spread[:, at])
-            re = jnp.zeros((8, chunk), F32)
-            im = jnp.zeros((8, chunk), F32)
-            for j in range(0, deep, 8):
-                br, bi = near[0, j : j + 8, at], near[1, j : j + 8, at]
-                wr, wi = wide[j : j + 8], wide[deep + j : deep + j + 8]
-                re += br * wr - bi * wi
-                im += br * wi + bi * wr
-            acc[0, :, at] = re
-            acc[1, :, at] = im
-
-        per = part // chunk
-        if it == 0:
-            for i in range(near_parts):
-                near_in[i].wait()
-                pl.loop(i * per, (i + 1) * per)(one)
-        else:
-            pl.loop(0, cells // chunk)(one)
+            lhs = left[pl.ds(pl.multiple_of(t * 16, 16), 16), :]
+            a = dot(lhs, block_h[0, :, at]) + dot(lhs, block_l[0, :, at])
+            b = dot(lhs, block_h[1, :, at]) + dot(lhs, block_l[1, :, at])
+            a = a[:8] + a[8:]
+            b = b[:8] + b[8:]
+            acc[0, :, at] = jnp.where(mine, jnp.where(upper, a, -b), zero)
+            acc[1, :, at] = jnp.where(mine, jnp.where(upper, b, a), zero)
+
+        pl.loop(0, cells // chunk, unroll=4)(one)
 
     def far_field(it, sends):
         for c in sends:
@@ -201,8 +203,6 @@
         got = dot(jnp.concatenate([q_h, q_l], axis=0), pick_far[:, :])
         got = got[: 2 * rank] + got[2 * rank :]
         qr, qi = got[:rank], got[rank:]
-        if it == 0:
-            coup_in.wait()
         sums = jnp.zeros((2 * rank * 8, LANES), F32)
         wide = 256
         for t in range(0, pairs, wide):
@@ -221,8 +221,6 @@
         z_high = z.astype(BF16).astype(F32)
         lane = lax.broadcasted_iota(jnp.int32, (2 * rank, LANES), 1) < half
         z = jnp.where(lane, z_high, z - z_high).astype(BF16)
-        if it == 0:
-            exp_in.wait()
         for t in range(0, cells, step):
             wide_z = dot(z, spread[:, t : t + step])
             zr, zi = wide_z[:rank], wide_z[rank:]
@@ -234,55 +232,84 @@
             new = jnp.concatenate([jnp.sum(x, axis=0, keepdims=True), jnp.sum(y, axis=0, keepdims=True)], axis=0)
             field[:, t : t + step] = adj[:, t : t + step] + new
 
+    def cut(t):
+        chunk = 4 * width
+        at = pl.ds(pl.multiple_of(t * chunk, chunk), chunk)
+        for ri in range(2):
+            for j in range(0, near_count * width, 16):
+                high, low = split(near[ri, j : j + 16, at])
+                block_h[ri, j : j + 16, at] = high
+                block_l[ri, j : j + 16, at] = low
+
+    def prepare():
+        list_in.wait()
+        local = list_ref[:, :] - me * clusters
+        r = lax.broadcasted_iota(jnp.int32, (4 * clusters, clusters), 0)
+        c = lax.broadcasted_iota(jnp.int32, (4 * clusters, clusters), 1)
+        cluster = ((r >> 4) << 2) + (r & 3)
+        own = onehot(c == cluster)
+        column = lax.broadcasted_iota(jnp.int32, (4 * clusters, 2 * LANES), 1)
+        row = lax.broadcasted_iota(jnp.int32, (4 * clusters, 2 * LANES), 0)
+        lbits = lines.bit_length() - 1
+        partner = ((column & (lines - 1)) << 1) + (column >> (lbits + 2))
+        same = ((row >> 2) & 3) == ((column >> lbits) & 3)
+        for k in range(near_count):
+            wanted = jnp.broadcast_to(local[k : k + 1, :], (LANES, clusters)).astype(F32).astype(BF16)
+            wanted = lax.dot_general(own, wanted, (((1,), (1,)), ((), ())), preferred_element_type=F32)
+            wanted = wanted.astype(jnp.int32)
+            wanted = jnp.concatenate([wanted, wanted], axis=1)
+            pick_near[k] = onehot(same & (partner == wanted))
+        owner_in.wait()
+        slot_in.wait()
+        source = owner_ref[:, :] * clusters + slot_ref[:, :]
+
+        @pl.loop(0, peers * clusters // 64)
+        def _(i):
+            r = lax.broadcasted_iota(jnp.int32, (64, pairs), 0) + i * 64
+            pick_far[pl.ds(pl.multiple_of(i * 64, 64), 64), :] = onehot(r == source)
+
+        r = lax.broadcasted_iota(jnp.int32, (pairs, LANES), 0) >> far_shift
+        c = lax.broadcasted_iota(jnp.int32, (pairs, LANES), 1) & (half - 1)
+        pair_sum[:, :] = onehot(r == c)
+
+        for i in range(near_parts):
+            near_in[i].wait()
+            pl.loop(i * (part // (4 * width)), (i + 1) * (part // (4 * width)))(cut)
+        coup_in.wait()
+        exp_in.wait()
+
     con_in.wait()
     adj_in.wait()
     field[:, :] = adj[:, :]
-    w = weigh()
     proj_in.wait()
-    project(w, 0)
-    pl.semaphore_wait(barrier, peers + freqs - 2)
-    sends = send(0)
-    everyone = sends
-
-    r = lax.broadcasted_iota(jnp.int32, (2 * LANES, LANES), 0)
-    lbits = lines.bit_length() - 1
-    cluster = ((r & (lines - 1)) << 1) + (r >> 7)
-    source_ri = (r >> lbits) & 1
-    local = list_ref[:, :] - me * clusters
-    local = jnp.concatenate([local, local], axis=1)
-    for ri in range(2):
-        for k in range(near_count):
-            b = ri * near_count + k
-            pick_near[:, b * LANES : (b + 1) * LANES] = onehot((cluster == local[k : k + 1, :]) & (source_ri == ri))
-    near_field(0)
-
-    source = owner_ref[:, :] * clusters + slot_ref[:, :]
-
-    @pl.loop(0, peers * clusters // 64)
-    def _(i):
-        r = lax.broadcasted_iota(jnp.int32, (64, pairs), 0) + i * 64
-        pick_far[pl.ds(pl.multiple_of(i * 64, 64), 64), :] = onehot(r == source)
-
-    r = lax.broadcasted_iota(jnp.int32, (pairs, LANES), 0) >> far_shift
-    c = lax.broadcasted_iota(jnp.int32, (pairs, LANES), 1) & (half - 1)
-    pair_sum[:, :] = onehot(r == c)
-
-    far_field(0, sends)
-    for it in range(1, ITERS):
-        w = weigh()
-        project(w, it)
+
+    @pl.loop(0, ITERS)
+    def _(it):
+        weigh()
+        project(it)
+
+        @pl.when(it == 0)
+        def _():
+            pl.semaphore_wait(barrier, peers + freqs - 2)
+
         sends = send(it)
-        everyone = everyone + sends
+
+        @pl.when(it == 0)
+        def _():
+            prepare()
+
         near_field(it)
         far_field(it, sends)
+        for c in sends:
+            c.wait_send()
 
     out_copy = pltpu.make_async_copy(field, out_hbm, out_sem)
     out_copy.start()
     back_in.wait()
     terms = back[:, :] * field[:, :]
-    terms = terms[0:1] + terms[1:2]
+    wbuf[0:1, :] = terms[0:1] + terms[1:2]
     for m in range(lines):
-        gbuf[0, m : m + 1, :] = terms[:, m * LANES : (m + 1) * LANES]
+        gbuf[0, m : m + 1, :] = wbuf[0:1, m * LANES : (m + 1) * LANES]
     gsends = []
     for d in range(1, freqs):
         copy = pltpu.make_async_remote_copy(
@@ -295,8 +322,6 @@
         )
         copy.start()
         gsends.append(copy)
-    for c in everyone:
-        c.wait_send()
     total = gbuf[0]
     for d, c in enumerate(gsends):
         c.wait_recv()
@@ -305,6 +330,18 @@
     for c in gsends:
         c.wait_send()
     out_copy.wait()
+
+
+def finish(a_ref, g_ref, a_out, g_out, a_buf, g_buf, sem):
+    inward = [pltpu.make_async_copy(a_ref, a_buf, sem.at[0]), pltpu.make_async_copy(g_ref, g_buf, sem.at[1])]
+    outward = [pltpu.make_async_copy(a_buf, a_out, sem.at[2]), pltpu.make_async_copy(g_buf, g_out, sem.at[3])]
+    for c in inward:
+        c.start()
+    for c, d in zip(inward, outward):
+        c.wait()
+        d.start()
+    for d in outward:
+        d.wait()
 
 
 def per_device(
@@ -328,7 +365,7 @@
     lines = cells // LANES
     near_parts = 4
     dims = (peers, freqs, clusters, cells, rank, near_count, pairs, near_parts)
-    hbm = pl.BlockSpec(memory_space=pl.ANY)
+    hbm = pl.BlockSpec(memory_space=pltpu.HBM)
     vmem = pl.BlockSpec(memory_space=pltpu.VMEM)
     deep = near_blocks.shape[2]
     adjoint, gradient = pl.pallas_call(
@@ -337,7 +374,7 @@
             jax.ShapeDtypeStruct((2, cells), F32),
             jax.ShapeDtypeStruct((lines, LANES), F32),
         ),
-        in_specs=[hbm, hbm, hbm, hbm, vmem, hbm, hbm, hbm, vmem, vmem],
+        in_specs=[hbm] * 10,
         out_specs=(hbm, vmem),
         scratch_shapes=[
             pltpu.VMEM((2, cells), F32),
@@ -347,17 +384,24 @@
             pltpu.VMEM((2, rank, cells), F32),
             pltpu.VMEM((2, rank, cells), F32),
             pltpu.VMEM((2, rank, rank, pairs), F32),
-            pltpu.VMEM((4 * lines, LANES), F32),
+            pltpu.VMEM((near_count, clusters), jnp.int32),
+            pltpu.VMEM((1, pairs), jnp.int32),
+            pltpu.VMEM((1, pairs), jnp.int32),
+            pltpu.VMEM((2 * lines, LANES), F32),
+            pltpu.VMEM((2, cells), F32),
             pltpu.VMEM((LANES, cells), BF16),
             pltpu.VMEM((cells, LANES), BF16),
-            pltpu.VMEM((2 * LANES, 2 * near_count * LANES), BF16),
+            pltpu.VMEM((near_count, 4 * clusters, 2 * LANES), BF16),
+            pltpu.VMEM((4 * clusters, deep), BF16),
+            pltpu.VMEM((2, deep, cells), BF16),
+            pltpu.VMEM((2, deep, cells), BF16),
             pltpu.VMEM((peers * clusters, pairs), BF16),
             pltpu.VMEM((pairs, LANES), BF16),
             pltpu.VMEM((2, 8, cells), F32),
             pltpu.VMEM((ITERS, peers, rank, LANES), F32),
             pltpu.VMEM((freqs, lines, LANES), F32),
             pltpu.VMEM((2, cells), F32),
-            pltpu.SemaphoreType.DMA((6,)),
+            pltpu.SemaphoreType.DMA((9,)),
             pltpu.SemaphoreType.DMA((near_parts,)),
             pltpu.SemaphoreType.DMA,
             pltpu.SemaphoreType.DMA((ITERS, peers)),
@@ -366,7 +410,7 @@
             pltpu.SemaphoreType.DMA((freqs,)),
         ],
         compiler_params=pltpu.CompilerParams(
-            collective_id=0, has_side_effects=True, vmem_limit_bytes=48 * 2**20
+            collective_id=0, has_side_effects=True, vmem_limit_bytes=60 * 2**20
         ),
     )(
         adj_source[0],
@@ -380,6 +424,18 @@
         far_owner.reshape(1, pairs),
         far_slot.reshape(1, pairs),
     )
+    adjoint, gradient = pl.pallas_call(
+        finish,
+        out_shape=(jax.ShapeDtypeStruct((2, cells), F32), jax.ShapeDtypeStruct((lines, LANES), F32)),
+        in_specs=[hbm] * 2,
+        out_specs=[hbm] * 2,
+        scratch_shapes=[
+            pltpu.VMEM((2, cells), F32),
+            pltpu.VMEM((lines, LANES), F32),
+            pltpu.SemaphoreType.DMA((4,)),
+        ],
+        compiler_params=pltpu.CompilerParams(vmem_limit_bytes=60 * 2**20),
+    )(adjoint, gradient)
     return adjoint[None], gradient.reshape(cells)
 
 

time: 31.3 us -> 23.6 us (0.75)
  local copies, waits for them, and re-layouts: 9.18 us -> 0 us
  Pallas kernels: 21 us -> 22.7 us
    unnamed x20 -> x0, local copies, waits for them, and re-layouts: 9.18 us -> none
    pallas_call x0 -> x1, Pallas kernels: none -> 1.41 us  [per_device(): pl.pallas_call(finish, out_shape=(jax.ShapeDtypeStruct((2, cells), F32),...]
    pallas_call x1, Pallas kernels: 21 us -> 21.3 us  [per_device(): pl.pallas_call(functools.partial(kernel, dims), out_shape=(jax.ShapeDtype...]
where the time goes in v1:
time: 23.6 us; the launch traced here: 23.4 us
  Pallas kernels  22.7 us (96%)
  between operations  0.64 us (3%)
    pallas_call x1, Pallas kernels, per_device(): pl.pallas_call(functools.partial(kernel, dims), out_shape=(jax.ShapeDtype...  21.3 us
    pallas_call x1, Pallas kernels, per_device(): pl.pallas_call(finish, out_shape=(jax.ShapeDtypeStruct((2, cells), F32),...  1.41 us

profile of v1, /device:TPU:0, one launch (start us, length us, event | category | flops | bytes accessed | tf_op | source)
XLA Modules:
  0.0 23.4 jit_solution(15899029141004515295)
XLA Ops:
  0.6 21.3 %shard_map.113 = (f32[2,4096]{1,0:T(2,128)}, f32[32,128]{1,0:T(8,128)}) custom-call(f32[2,4096]{1,0:T(2,128)} %bitcast.15, f32[1,4096]{1,0:T(1,128)} %con_hbm.1, f32[2,4096]{1,0:T(2,128)} %bitcast.16, f32[2,192,4096]{2,1,0:T(8,128)} %bitcast.11, s32[3,64]{1,0:T(4,128)} %bitcast.19, f32[2,16,4096]{2,1,0:T(8,128)} %bitcast.13, f32[2,16,4096]{2,1,0:T(8,128)} %bitcast.14, ...), custom_call_target="tpu_custom_call" | custom-call | tf_op jit(solution)/shard_map/pallas_call | solution.py:371
  22.0 1.4 %shard_map.114 = (f32[2,4096]{1,0:T(2,128)}, f32[32,128]{1,0:T(8,128)}) custom-call(f32[2,4096]{1,0:T(2,128)} %get-tuple-element.6.a_ref, f32[32,128]{1,0:T(8,128)} %get-tuple-element.7.g_ref), custom_call_target="tpu_custom_call" | custom-call | tf_op jit(solution)/shard_map/pallas_call | solution.py:427

commit v2 on v1

--- a/solution.py
+++ b/solution.py
@@ -117,9 +117,6 @@
 
     step = 512
     for t in range(0, cells, step):
-        r = lax.broadcasted_iota(jnp.int32, (LANES, step), 0) & (half - 1)
-        c = (lax.broadcasted_iota(jnp.int32, (LANES, step), 1) + t) >> shift
-        spread[:, t : t + step] = onehot(r == c)
         r = (lax.broadcasted_iota(jnp.int32, (step, LANES), 0) + t) >> shift
         c = lax.broadcasted_iota(jnp.int32, (step, LANES), 1) & (half - 1)
         collect[t : t + step, :] = onehot(r == c)
@@ -242,6 +239,10 @@
                 block_l[ri, j : j + 16, at] = low
 
     def prepare():
+        for t in range(0, cells, step):
+            r = lax.broadcasted_iota(jnp.int32, (LANES, step), 0) & (half - 1)
+            c = (lax.broadcasted_iota(jnp.int32, (LANES, step), 1) + t) >> shift
+            spread[:, t : t + step] = onehot(r == c)
         list_in.wait()
         local = list_ref[:, :] - me * clusters
         r = lax.broadcasted_iota(jnp.int32, (4 * clusters, clusters), 0)

time: 23.6 us -> 23.6 us (level)
  no operation moved by 1% of the time
where the time goes in v2:
time: 23.6 us; the launch traced here: 23.4 us
  Pallas kernels  22.7 us (96%)
  between operations  0.64 us (3%)
    pallas_call x1, Pallas kernels, per_device(): pl.pallas_call(functools.partial(kernel, dims), out_shape=(jax.ShapeDtype...  21.3 us
    pallas_call x1, Pallas kernels, per_device(): pl.pallas_call(finish, out_shape=(jax.ShapeDtypeStruct((2, cells), F32),...  1.41 us

profile of v2, /device:TPU:0, one launch (start us, length us, event | category | flops | bytes accessed | tf_op | source)
XLA Modules:
  0.0 23.4 jit_solution(1812298294346685041)
XLA Ops:
  0.6 21.3 %shard_map.113 = (f32[2,4096]{1,0:T(2,128)}, f32[32,128]{1,0:T(8,128)}) custom-call(f32[2,4096]{1,0:T(2,128)} %bitcast.15, f32[1,4096]{1,0:T(1,128)} %con_hbm.1, f32[2,4096]{1,0:T(2,128)} %bitcast.16, f32[2,192,4096]{2,1,0:T(8,128)} %bitcast.11, s32[3,64]{1,0:T(4,128)} %bitcast.19, f32[2,16,4096]{2,1,0:T(8,128)} %bitcast.13, f32[2,16,4096]{2,1,0:T(8,128)} %bitcast.14, ...), custom_call_target="tpu_custom_call" | custom-call | tf_op jit(solution)/shard_map/pallas_call | solution.py:372
  22.0 1.4 %shard_map.114 = (f32[2,4096]{1,0:T(2,128)}, f32[32,128]{1,0:T(8,128)}) custom-call(f32[2,4096]{1,0:T(2,128)} %get-tuple-element.6.a_ref, f32[32,128]{1,0:T(8,128)} %get-tuple-element.7.g_ref), custom_call_target="tpu_custom_call" | custom-call | tf_op jit(solution)/shard_map/pallas_call | solution.py:428
